TPU v7x, 32 devices: a whole 2x2x4 slice. The times are simulated.
32 devices in a mesh: parts: 2 (over x), leaf: 16 (over z, y, core).
Axes of the slice: x: 2, y: 2, z: 4, core: 2. Of those that a mesh axis runs over, the one named last changes fastest.
Arguments:
- root_cov: float32 [6144, 3072], P(('parts', 'leaf')), parts along dimension 0, may hold values from -40 to 40, as said below
- panel_one: bfloat16 [6144, 2048], P(('parts', 'leaf')), parts along dimension 0, may hold values from -0.078125 to 0.078125
- pattern_one: int32 [24, 16], replicated, may hold values 0 or 1
- inv_one: float32 [4096, 2048], P('parts', 'leaf'), parts along dimension 0, may hold values from -40 to 40, as said below
- panel_parent: bfloat16 [4096, 1024], P(('parts', 'leaf')), parts along dimension 0, may hold values from -0.0625 to 0.0625
- panel_root: bfloat16 [6144, 1024], P(('parts', 'leaf')), parts along dimension 0, may hold values from -0.0625 to 0.0625
- pattern_two: int32 [40, 8], replicated, may hold values 0 or 1
- inv_two: float32 [2048, 1024], P('parts', 'leaf'), parts along dimension 0, may hold values from -40 to 40, as said below
Outputs:
- cross_one: float32 [6144, 2048], P(('parts', 'leaf')), parts along dimension 0
- cov_one: float32 [4096, 2048], P('parts', 'leaf'), parts along dimension 0
- cross_two_parent: float32 [4096, 1024], P(('parts', 'leaf')), parts along dimension 0
- cross_two_root: float32 [6144, 1024], P(('parts', 'leaf')), parts along dimension 0
- cov_two: float32 [2048, 1024], P('parts', 'leaf'), parts along dimension 0
There are 2 independent parts, one for each index of `parts`. A program takes and returns all parts, laid end to end along the dimension named above; an argument that names none is the same for every part. Nothing has to cross between parts.
Inputs may be any that keep to these rules, and one draw needn't show every extreme that they name: `root_cov`: symmetric. `inv_one`: symmetric. `inv_two`: symmetric.
All inputs are finite; a program needn't handle non-finite values.
Results may differ from a plain program's by a relative error of at most 0.00095.
Values may be sent and summed in bfloat16 or wider, within the bound.
A program may use at most 128 MiB of HBM per device.

v0:
```python
import jax
import jax.numpy as jnp
from jax import lax
from jax.sharding import PartitionSpec as P

BLOCK = 128


def product(left, right):
    return jnp.dot(left, right, precision=lax.Precision.HIGHEST, preferred_element_type=jnp.float32)


def contract_rows(left, right):
    return lax.dot_general(
        left,
        right,
        (((0,), (0,)), ((), ())),
        precision=lax.Precision.HIGHEST,
        preferred_element_type=jnp.float32,
    )


def pattern_rows(pattern, first_row, count_rows):
    row_index = first_row + jnp.arange(count_rows, dtype=jnp.int32)
    tile_index = row_index // BLOCK
    choose = (tile_index[:, None] == jnp.arange(pattern.shape[0], dtype=jnp.int32)[None, :]).astype(
        jnp.float32
    )
    picked = jnp.dot(choose, pattern.astype(jnp.float32))
    return jnp.repeat(picked, BLOCK, axis=1) > 0.5


def per_device(
    root_cov, panel_one, pattern_one, inv_one, panel_parent, panel_root, pattern_two, inv_two
):
    position = lax.axis_index("leaf")
    root_rows = root_cov.shape[0]
    parent_rows = panel_parent.shape[0]
    parent_width = panel_one.shape[1]
    keep_one = pattern_rows(pattern_one, position * root_rows, root_rows)
    masked_one = jnp.where(keep_one, panel_one, jnp.zeros_like(panel_one))
    keep_parent = pattern_rows(pattern_two, position * parent_rows, parent_rows)
    masked_parent = jnp.where(keep_parent, panel_parent, jnp.zeros_like(panel_parent))
    keep_root = pattern_rows(pattern_two, parent_width + position * root_rows, root_rows)
    masked_root = jnp.where(keep_root, panel_root, jnp.zeros_like(panel_root))
    full_one, full_parent, full_root = (
        lax.all_gather(masked_one, "leaf", axis=0, tiled=True),
        lax.all_gather(masked_parent, "leaf", axis=0, tiled=True),
        lax.all_gather(masked_root, "leaf", axis=0, tiled=True),
    )
    one_wide = full_one.astype(jnp.float32)
    cross_rows = -product(root_cov, one_wide)
    cross_cols = lax.all_to_all(cross_rows, "leaf", split_axis=1, concat_axis=0, tiled=True)
    cov_cols = inv_one - contract_rows(one_wide, cross_cols)
    parent_wide = full_parent.astype(jnp.float32)
    root_wide = full_root.astype(jnp.float32)
    upper_rows = -(contract_rows(cov_cols, parent_wide) + contract_rows(cross_cols, root_wide))
    lower_rows = -(product(cross_rows, parent_wide) + product(root_cov, root_wide))
    upper_cols, lower_cols = (
        lax.all_to_all(
            upper_rows.astype(jnp.bfloat16), "leaf", split_axis=1, concat_axis=0, tiled=True
        ).astype(upper_rows.dtype),
        lax.all_to_all(
            lower_rows.astype(jnp.bfloat16), "leaf", split_axis=1, concat_axis=0, tiled=True
        ).astype(lower_rows.dtype),
    )
    child_cov = inv_two - (
        contract_rows(parent_wide, upper_cols) + contract_rows(root_wide, lower_cols)
    )
    return (cross_rows, cov_cols, upper_rows, lower_rows, child_cov)


def solution(mesh):
    placed = (
        P(("parts", "leaf"), None),
        P(("parts", "leaf"), None),
        P(),
        P("parts", "leaf"),
        P(("parts", "leaf"), None),
        P(("parts", "leaf"), None),
        P(),
        P("parts", "leaf"),
    )
    return jax.shard_map(
        per_device,
        mesh=mesh,
        in_specs=placed,
        out_specs=(
            P(("parts", "leaf"), None),
            P("parts", "leaf"),
            P(("parts", "leaf"), None),
            P(("parts", "leaf"), None),
            P("parts", "leaf"),
        ),
        check_vma=False,
    )
```

profile of v0, /device:TPU:0, one launch (start us, length us, event | category | flops | bytes accessed | tf_op | source)
XLA Modules:
  0.0 323.5 jit_solution(17817469250981125496)
XLA Ops:
  7.2 0.0 copy-start
  7.2 0.0 copy-start.6
  7.2 0.0 all-gather.4.cloned.1.call-start
  7.3 1.1 convolution_compare_fusion
  8.3 0.1 copy.16
  8.5 0.6 broadcast_in_dim.24
  9.1 2.2 bitcast_select_fusion
  11.3 0.0 all-gather.4.cloned.1.call-update
  11.3 0.0 all-gather.8.cloned.1.call-start
  11.4 0.9 convolution_compare_fusion.1
  12.3 0.2 copy.19
  12.5 0.3 broadcast_in_dim.28
  12.7 1.9 bitcast_select_fusion.1
  14.6 0.0 all-gather.8.cloned.1.call-update
  14.6 0.0 all-gather.6.cloned.1.call-start
  14.7 0.0 copy-done.6
  14.7 0.2 convolution_compare_fusion.2
  14.9 0.1 copy.18
  15.0 0.2 broadcast_in_dim.26
  15.3 0.0 copy-done.5
  15.3 0.8 bitcast_select_fusion.2
  16.0 0.0 all-gather.6.cloned.1.call-update
  16.1 98.9 %all-gather.4.cloned.1.call-done = bf16[3072,2048]{1,0:T(8,128)(2,1)} async-done(((bf16[192,2048]{1,0:T(8,128)(2,1)}), bf16[3072,2048]{1,0:T(8,128)(2,1)}) %all-gather.4.cloned.1.call-update) | async-done | bytes 12582928 | tf_op jit(solution)/shard_map/all_gather | solution.py:47
  114.9 10.5 %convolution_negate_fusion = f32[2048,192]{0,1:T(8,128)S(1)} fusion(bf16[3072,2048]{1,0:T(8,128)(2,1)} %all-gather.4.cloned.1.call-done, f32[192,3072]{1,0:T(8,128)S(1)} %copy-done), kind=kOutput, calls=%fused_computation | convolution fusion | flops 14495907840 | bytes 16515072 | tf_op jit(solution)/shard_map/dot_general | solution.py:10
  125.4 0.0 copy-start.2
  125.4 1.1 copy-done.2
  126.6 1.4 copy_bitcast_fusion
  128.0 4.4 %all-to-all-start = ((f32[192,16,128]{2,0,1:T(8,128)}), f32[192,16,128]{2,0,1:T(8,128)}, u32[]{:S(2)}, u32[]{:S(2)}) async-start(f32[192,16,128]{2,0,1:T(8,128)} %copy_bitcast_fusion), calls=%async_computation | async-start | bytes 3145728 | tf_op jit(solution)/shard_map/all_to_all | solution.py:53
  132.4 69.2 %all-gather.8.cloned.1.call-done = bf16[3072,1024]{1,0:T(8,128)(2,1)} async-done(((bf16[192,1024]{1,0:T(8,128)(2,1)}), bf16[3072,1024]{1,0:T(8,128)(2,1)}) %all-gather.8.cloned.1.call-update) | async-done | bytes 6291472 | tf_op jit(solution)/shard_map/all_gather | solution.py:49
  201.6 6.0 %convolution_bitcast_fusion = f32[192,1024]{1,0:T(8,128)S(1)} fusion(bf16[3072,1024]{1,0:T(8,128)(2,1)} %all-gather.8.cloned.1.call-done, f32[192,3072]{1,0:T(8,128)S(1)} %copy-done), kind=kOutput, calls=%fused_computation.4 | convolution fusion | flops 7247757312 | bytes 9437184 | tf_op jit(solution)/shard_map/dot_general | solution.py:10
  207.6 46.2 %all-gather.6.cloned.1.call-done = bf16[2048,1024]{1,0:T(8,128)(2,1)} async-done(((bf16[128,1024]{1,0:T(8,128)(2,1)}), bf16[2048,1024]{1,0:T(8,128)(2,1)}) %all-gather.6.cloned.1.call-update) | async-done | bytes 4194320 | tf_op jit(solution)/shard_map/all_gather | solution.py:48
  253.8 6.2 %fusion.13 = (bf16[192,1024]{1,0:T(8,128)(2,1)S(1)}, f32[192,1024]{1,0:T(8,128)}) fusion(f32[192,1024]{1,0:T(8,128)S(1)} %convolution_bitcast_fusion, f32[2048,192]{0,1:T(8,128)} %copy-done.2, bf16[2048,1024]{1,0:T(8,128)(2,1)} %all-gather.6.cloned.1.call-done), kind=kOutput, calls=%fused_computation.41 | convolution fusion | flops 4832428032 | bytes 7733248 | tf_op jit(solution)/shard_map/dot_general | solution.py:10
  260.1 1.0 copy.22
  261.1 0.0 all-to-all-done
  261.1 4.4 %all-to-all-start.2 = ((bf16[192,16,64]{0,2,1:T(8,128)(2,1)}), bf16[192,16,64]{0,2,1:T(8,128)(2,1)}, u32[]{:S(2)}, u32[]{:S(2)}) async-start(bf16[192,16,64]{0,2,1:T(8,128)(2,1)} %bitcast.7), calls=%async_computation.2 | async-start | bytes 1048576 | tf_op jit(solution)/shard_map/all_to_all | solution.py:63
  265.5 17.0 %convolution_subtract_fusion = f32[2048,128]{1,0:T(8,128)S(1)} fusion(f32[2048,128]{1,0:T(8,128)} %param.11, bf16[3072,2048]{1,0:T(8,128)(2,1)} %all-gather.4.cloned.1.call-done, f32[3072,128]{1,0:T(8,128)} %bitcast.2), kind=kOutput, calls=%fused_computation.1 | convolution fusion | flops 9663938560 | bytes 16252928 | tf_op jit(solution)/shard_map/dot_general | solution.py:14
  282.5 0.0 copy-start.3
  282.5 6.2 %fusion.14 = f32[128,1024]{1,0:T(8,128)S(1)} fusion(f32[3072,128]{1,0:T(8,128)} %bitcast.2, bf16[3072,1024]{1,0:T(8,128)(2,1)} %all-gather.8.cloned.1.call-done), kind=kOutput, calls=%fused_computation.42 | convolution fusion | flops 4831838208 | bytes 8388608 | tf_op jit(solution)/shard_map/dot_general | solution.py:14
  288.7 2.9 fusion.12
  291.7 1.8 copy.20
  293.5 0.0 all-to-all-done.2
  293.5 5.7 %all-to-all-start.1 = ((bf16[128,16,64]{0,2,1:T(8,128)(2,1)}), bf16[128,16,64]{0,2,1:T(8,128)(2,1)S(1)}, u32[]{:S(2)}, u32[]{:S(2)}) async-start(bf16[128,16,64]{0,2,1:T(8,128)(2,1)} %bitcast.5), calls=%async_computation.1 | async-start | bytes 524288 | tf_op jit(solution)/shard_map/all_to_all | solution.py:60
  299.2 1.3 copy.23
  300.6 0.5 all_to_all.53
  301.1 0.0 copy-start.4
  301.1 8.2 %all-to-all-done.1 = bf16[128,16,64]{0,2,1:T(8,128)(2,1)S(1)} async-done(((bf16[128,16,64]{0,2,1:T(8,128)(2,1)}), bf16[128,16,64]{0,2,1:T(8,128)(2,1)S(1)}, u32[]{:S(2)}, u32[]{:S(2)}) %all-to-all-start.1) | async-done | bytes 262176 | tf_op jit(solution)/shard_map/all_to_all | solution.py:60
  309.3 3.0 fusion.3
  312.3 4.7 %fusion.2 = f32[1024,64]{0,1:T(8,128)} fusion(f32[1024,64]{0,1:T(8,128)S(1)} %copy-done.4, f32[1024,64]{0,1:T(8,128)S(1)} %fusion.3, bf16[3072,64]{0,1:T(8,128)(2,1)S(1)} %all_to_all.53, bf16[3072,1024]{1,0:T(8,128)(2,1)} %all-gather.8.cloned.1.call-done), kind=kOutput, calls=%fused_computation.10 | convolution fusion | flops 402784256 | bytes 7471104 | tf_op jit(solution)/shard_map/dot_general | solution.py:14
  (9 shorter events, 0.0 us)
Async XLA Ops:
  7.2 107.8 %copy-start = (f32[192,3072]{1,0:T(8,128)S(1)}, f32[192,3072]{1,0:T(8,128)}, u32[]{:S(2)}) copy-start(f32[192,3072]{1,0:T(8,128)} %param.8) | copy-start | bytes 7077892
  7.2 7.5 %copy-start.6 = (s32[40,8]{0,1:T(8,128)S(1)}, s32[40,8]{0,1:T(8,128)}, u32[]{:S(2)}) copy-start(s32[40,8]{0,1:T(8,128)} %param.14) | copy-start | bytes 3844
  7.2 8.1 %copy-start.5 = (bf16[128,1024]{1,0:T(8,128)(2,1)S(1)}, bf16[128,1024]{1,0:T(8,128)(2,1)}, u32[]{:S(2)}) copy-start(bf16[128,1024]{1,0:T(8,128)(2,1)} %param.12) | copy-start | bytes 786436
  7.2 107.7 %all-gather.4.cloned.1.call-start = ((), (), s32[]{:S(2)}) async-start(), calls=%async_computation.3 | async-start | bytes 13369344 | tf_op jit(solution)/shard_map/all_gather | solution.py:47
  11.3 190.3 %all-gather.8.cloned.1.call-start = ((), (), s32[]{:S(2)}) async-start(), calls=%async_computation.5 | async-start | bytes 6684672 | tf_op jit(solution)/shard_map/all_gather | solution.py:49
  14.6 239.2 %all-gather.6.cloned.1.call-start = ((), (), s32[]{:S(2)}) async-start(), calls=%async_computation.4 | async-start | bytes 4456448 | tf_op jit(solution)/shard_map/all_gather | solution.py:48
  125.4 1.1 copy-start.2
  128.0 133.1 %all-to-all-start = ((f32[192,16,128]{2,0,1:T(8,128)}), f32[192,16,128]{2,0,1:T(8,128)}, u32[]{:S(2)}, u32[]{:S(2)}) async-start(f32[192,16,128]{2,0,1:T(8,128)} %copy_bitcast_fusion), calls=%async_computation | async-start | bytes 3145728 | tf_op jit(solution)/shard_map/all_to_all | solution.py:53
  261.1 32.4 %all-to-all-start.2 = ((bf16[192,16,64]{0,2,1:T(8,128)(2,1)}), bf16[192,16,64]{0,2,1:T(8,128)(2,1)}, u32[]{:S(2)}, u32[]{:S(2)}) async-start(bf16[192,16,64]{0,2,1:T(8,128)(2,1)} %bitcast.7), calls=%async_computation.2 | async-start | bytes 1048576 | tf_op jit(solution)/shard_map/all_to_all | solution.py:63
  282.5 6.3 %copy-start.3 = (f32[2048,128]{1,0:T(8,128)}, f32[2048,128]{1,0:T(8,128)S(1)}, u32[]{:S(2)}) copy-start(f32[2048,128]{1,0:T(8,128)S(1)} %convolution_subtract_fusion) | copy-start | bytes 3145732
  282.5 6.3 %copy-start.1 = (bf16[2048,1024]{1,0:T(8,128)(2,1)S(1)}, bf16[2048,1024]{1,0:T(8,128)(2,1)}, u32[]{:S(2)}) copy-start(bf16[2048,1024]{1,0:T(8,128)(2,1)} %all-gather.6.cloned.1.call-done) | copy-start | bytes 12582916
  293.5 15.8 %all-to-all-start.1 = ((bf16[128,16,64]{0,2,1:T(8,128)(2,1)}), bf16[128,16,64]{0,2,1:T(8,128)(2,1)S(1)}, u32[]{:S(2)}, u32[]{:S(2)}) async-start(bf16[128,16,64]{0,2,1:T(8,128)(2,1)} %bitcast.5), calls=%async_computation.1 | async-start | bytes 524288 | tf_op jit(solution)/shard_map/all_to_all | solution.py:60
  301.1 11.2 %copy-start.4 = (f32[1024,64]{0,1:T(8,128)S(1)}, f32[1024,64]{0,1:T(8,128)}, u32[]{:S(2)}) copy-start(f32[1024,64]{0,1:T(8,128)} %param.15) | copy-start | bytes 786436
Sparse Core Ops, SparseCore 0:
  11.4 103.4 all-gather.3
  117.8 83.8 all-gather.7
  204.4 49.4 all-gather.5
where the time goes:
time: 324 us
  waiting for transfers between devices  223 us (69%)
  matrix products  58.7 us (18%)
  starting transfers between devices  14.7 us (5%)
  between operations  14 us (4%)
  local copies, waits for them, and re-layouts  8.76 us (3%)
  other arithmetic  4.88 us (2%)
    all_gather x1, waiting for transfers between devices, per_device(): lax.all_gather(masked_one, 'leaf', axis=0, tiled=True)  98.9 us
    all_gather x1, waiting for transfers between devices, per_device(): lax.all_gather(masked_root, 'leaf', axis=0, tiled=True)  69.2 us
    all_gather x1, waiting for transfers between devices, per_device(): lax.all_gather(masked_parent, 'leaf', axis=0, tiled=True)  46.2 us
    dot_general x5, matrix products, contract_rows(): lax.dot_general(left, right, (((0,), (0,)), ((), ())), precision=lax.Prec...  33.9 us
    dot_general x3, matrix products, product(): jnp.dot(left, right, precision=lax.Precision.HIGHEST, preferred_element_t...  22.7 us
    all_to_all x1, waiting for transfers between devices, per_device(): lax.all_to_all(upper_rows.astype(jnp.bfloat16), 'leaf', split_axis=1, con...  8.15 us
  transfers between devices with their start and end apart: 6, of which 4 were waited for; matrix products, arithmetic and copies ran while one was open for 18% of the time, Pallas kernels for 0%

commit v1 on v0

--- a/solution.py
+++ b/solution.py
@@ -1,6 +1,8 @@
 import jax
 import jax.numpy as jnp
 from jax import lax
+from jax.experimental import pallas as pl
+from jax.experimental.pallas import tpu as pltpu
 from jax.sharding import PartitionSpec as P
 
 BLOCK = 128
@@ -70,6 +72,293 @@
     return (cross_rows, cov_cols, upper_rows, lower_rows, child_cov)
 
 
+PLANES = 4
+GROUP = PLANES * 4
+COLUMN_TILE = 512
+CUTS = (2, 1, 1)
+CROSS_SCALE = 4.0
+
+
+def split_rows(values):
+    high = values.astype(jnp.bfloat16)
+    low = (values - high.astype(jnp.float32)).astype(jnp.bfloat16)
+    return high, low
+
+
+def split_wide(values):
+    high = lax.reduce_precision(values, 8, 7)
+    return high.astype(jnp.bfloat16), (values - high).astype(jnp.bfloat16)
+
+
+def gather_steps(shards, patterns, tiles_before, fulls, outs, cuts, send_sem, recv_sem, out_sem, use):
+    leaf = lax.axis_index("leaf")
+    plane, side, core = leaf // 4, (leaf // 2) % 2, leaf % 2
+
+    def device(z, y, c):
+        return z * 4 + y * 2 + c
+
+    up, down = device(plane + 1, side, core), device(plane - 1, side, core)
+    across, twin = device(plane, 1 - side, core), device(plane, side, 1 - core)
+    barrier = pltpu.get_barrier_semaphore()
+    has_up, has_down = plane < PLANES - 1, plane > 0
+    for there, target in ((has_up, up), (has_down, down), (None, across), (None, twin)):
+        def greet(target=target):
+            pl.semaphore_signal(
+                barrier, inc=1, device_id={"leaf": target}, device_id_type=pl.DeviceIdType.MESH
+            )
+        if there is None:
+            greet()
+        else:
+            pl.when(there)(greet)
+
+    def rows_of(index, origin, count=1):
+        height = shards[index].shape[0]
+        return pl.ds(pl.multiple_of(origin * height, 16), height * count)
+
+    for index, shard in enumerate(shards):
+        height = shard.shape[0]
+        tiles = patterns[index].shape[0]
+        row = lax.broadcasted_iota(jnp.int32, (height, tiles), 0) + leaf * height
+        tile = lax.broadcasted_iota(jnp.int32, (height, tiles), 1) - tiles_before[index]
+        inside = (row >= tile * BLOCK) & (row < (tile + 1) * BLOCK)
+        keep = jnp.dot(
+            inside.astype(jnp.float32), patterns[index][...], preferred_element_type=jnp.float32
+        )
+        wide = shard[...].astype(jnp.float32)
+        fulls[index][rows_of(index, leaf), :] = jnp.where(keep > 0.5, wide, 0.0).astype(jnp.bfloat16)
+    pl.semaphore_wait(barrier, 2 + has_up.astype(jnp.int32) + has_down.astype(jnp.int32))
+
+    started = []
+
+    pieces = []
+    for index, (full, parts) in enumerate(zip(fulls, cuts)):
+        width = full.shape[1] // parts
+        pieces += [(index, part * width, width) for part in range(parts)]
+
+    def piece_copy(piece, origin, target, sem):
+        index, first, width = pieces[piece]
+        here = fulls[index].at[rows_of(index, origin), pl.ds(first, width)]
+        return pltpu.make_async_remote_copy(
+            src_ref=here,
+            dst_ref=here,
+            send_sem=send_sem.at[sem],
+            recv_sem=recv_sem.at[piece, origin],
+            device_id={"leaf": target},
+            device_id_type=pl.DeviceIdType.MESH,
+        )
+
+    def relay(origin, targets, there=None, received=True):
+        for piece in range(len(pieces)):
+            if received:
+                def wait(piece=piece):
+                    piece_copy(piece, origin, twin, 0).wait_recv()
+                wait() if there is None else pl.when(there)(wait)
+            for target, when in targets:
+                copy = piece_copy(piece, origin, target, len(started))
+                started.append((when, copy))
+                copy.start() if when is None else pl.when(when)(copy.start)
+
+    stored = []
+
+    def chip(z, y, there):
+        def work():
+            relay(device(z, y, 1 - core), ())
+            for index, (full, out) in enumerate(zip(fulls, outs)):
+                rows = rows_of(index, device(z, y, 0), 2)
+                pltpu.make_async_copy(full.at[rows, :], out.at[rows, :], out_sem.at[index, z * 2 + y]).start()
+            use(z * 2 + y)
+        stored.append((there, z, y))
+        if there is None:
+            work()
+        else:
+            pl.when(there)(work)
+
+    own = device(plane, side, core)
+    relay(own, ((up, has_up), (down, has_down), (across, None), (twin, None)), received=False)
+
+    def from_across(z, there):
+        origin = device(z, 1 - side, core)
+        onward = core == 1 if there is None else there & (core == 1)
+        targets = (
+            (down, onward & has_down & (z == PLANES - 1)),
+            (up, onward & has_up & (z == 0)),
+            (twin, there),
+        )
+        relay(origin, targets, there)
+
+    for step in range(1, PLANES + 1):
+        if step < PLANES:
+            for z, there, onward, more in (
+                (plane - step, plane - step >= 0, up, has_up),
+                (plane + step, plane + step <= PLANES - 1, down, has_down),
+            ):
+                origin = device(z, side, core)
+                far = there & ((core == 0) | ((z > 0) & (z < PLANES - 1)))
+                relay(origin, ((onward, there & more), (across, far), (twin, there)), there)
+        back = step - 1
+        if back == 0:
+            from_across(plane, None)
+            chip(plane, side, None)
+            chip(plane, 1 - side, None)
+        else:
+            near = (
+                (plane - back, plane - back >= 0),
+                (plane + back, plane + back <= PLANES - 1),
+            )
+            for z, there in near:
+                from_across(z, there)
+            for z, there in near:
+                chip(z, side, there)
+                chip(z, 1 - side, there)
+
+    for there, copy in started:
+        if there is None:
+            copy.wait_send()
+        else:
+            pl.when(there)(copy.wait_send)
+    for there, z, y in stored:
+        def finish(z=z, y=y):
+            for index, (full, out) in enumerate(zip(fulls, outs)):
+                rows = rows_of(index, device(z, y, 0), 2)
+                pltpu.make_async_copy(full.at[rows, :], out.at[rows, :], out_sem.at[index, z * 2 + y]).wait()
+        if there is None:
+            finish()
+        else:
+            pl.when(there)(finish)
+
+
+def add_products(stacked, start, depth, full, full_start, total):
+    height = total.shape[0]
+    left = stacked[:, pl.ds(pl.multiple_of(start, BLOCK), depth)]
+
+    def tile(step, carry):
+        columns = pl.ds(pl.multiple_of(step * COLUMN_TILE, COLUMN_TILE), COLUMN_TILE)
+        both = jnp.dot(
+            left,
+            full[pl.ds(pl.multiple_of(full_start, 16), depth), columns],
+            preferred_element_type=jnp.float32,
+        )
+        total[:, columns] -= both[:height] + both[height:]
+        return carry
+
+    lax.fori_loop(0, total.shape[1] // COLUMN_TILE, tile, 0)
+
+
+def fill_split(stacked, values):
+    height = values.shape[0]
+    high, low = split_rows(values[...])
+    stacked[:height, :] = high
+    stacked[height:, :] = low
+
+
+def gather_kernel(
+    root, one_shard, root_shard, parent_shard, one_pattern, two_pattern,
+    cross, lower, one_out, root_out, parent_out,
+    one_full, root_full, parent_full, stacked, cross_stacked, send_sem, recv_sem, out_sem,
+):
+    depth, width = 2 * root_shard.shape[0], parent_full.shape[0]
+    fill_split(stacked, root)
+    cross[...] = jnp.zeros_like(cross)
+    lower[...] = jnp.zeros_like(lower)
+
+    def use(block):
+        add_products(stacked, block * depth, depth, one_full, block * depth, cross)
+        add_products(stacked, block * depth, depth, root_full, block * depth, lower)
+
+    gather_steps(
+        (one_shard, root_shard, parent_shard),
+        (one_pattern, two_pattern, two_pattern),
+        (0, width // BLOCK, 0),
+        (one_full, root_full, parent_full),
+        (one_out, root_out, parent_out),
+        CUTS, send_sem, recv_sem, out_sem, use,
+    )
+    fill_split(cross_stacked, cross)
+    add_products(cross_stacked, 0, width, parent_full, 0, lower)
+
+
+def vmem(count):
+    return [pl.BlockSpec(memory_space=pltpu.VMEM)] * count
+
+
+def semaphores(arrays, pieces):
+    return [
+        pltpu.SemaphoreType.DMA((48 * pieces,)),
+        pltpu.SemaphoreType.DMA((pieces, GROUP)),
+        pltpu.SemaphoreType.DMA((arrays, GROUP // 2)),
+    ]
+
+
+def params(collective_id):
+    return pltpu.CompilerParams(
+        collective_id=collective_id, has_side_effects=True, vmem_limit_bytes=54 * 1024 * 1024
+    )
+
+
+def estimate(flops, nbytes):
+    return pl.CostEstimate(flops=flops, bytes_accessed=nbytes, transcendentals=0)
+
+
+def contract_split(left, right):
+    return lax.dot_general(
+        left, right, (((0,), (0,)), ((), ())), preferred_element_type=jnp.float32
+    )
+
+
+def per_device_kernels(
+    root_cov, panel_one, pattern_one, inv_one, panel_parent, panel_root, pattern_two, inv_two
+):
+    rows, order = root_cov.shape
+    parent_width, child_width = panel_one.shape[1], panel_root.shape[1]
+    bf16, f32 = jnp.bfloat16, jnp.float32
+    any_space = pl.BlockSpec(memory_space=pl.ANY)
+    spread_one = jnp.repeat(pattern_one.astype(f32), BLOCK, axis=1)
+    spread_two = jnp.repeat(pattern_two.astype(f32), BLOCK, axis=1)
+    cross_rows, lower_rows, full_one, full_root, full_parent = pl.pallas_call(
+        gather_kernel,
+        out_shape=(
+            jax.ShapeDtypeStruct((rows, parent_width), f32),
+            jax.ShapeDtypeStruct((rows, child_width), f32),
+            jax.ShapeDtypeStruct((order, parent_width), bf16),
+            jax.ShapeDtypeStruct((order, child_width), bf16),
+            jax.ShapeDtypeStruct((parent_width, child_width), bf16),
+        ),
+        in_specs=vmem(6),
+        out_specs=(*vmem(2), any_space, any_space, any_space),
+        scratch_shapes=[
+            pltpu.VMEM((order, parent_width), bf16),
+            pltpu.VMEM((order, child_width), bf16),
+            pltpu.VMEM((parent_width, child_width), bf16),
+            pltpu.VMEM((2 * rows, order), bf16),
+            pltpu.VMEM((2 * rows, parent_width), bf16),
+        ] + semaphores(3, sum(CUTS)),
+        compiler_params=params(0),
+        cost_estimate=estimate(4 * rows * order * (parent_width + child_width), 300_000_000),
+        name="gather_panels",
+    )(root_cov, panel_one, panel_root, panel_parent, spread_one, spread_two)
+    assert 3.125 * order * CROSS_SCALE < 65504
+    cross_cols = lax.all_to_all(
+        (cross_rows * CROSS_SCALE).astype(jnp.float16), "leaf", split_axis=1, concat_axis=0, tiled=True
+    ).astype(f32) * (1.0 / CROSS_SCALE)
+    lower_cols = lax.all_to_all(
+        lower_rows.astype(bf16), "leaf", split_axis=1, concat_axis=0, tiled=True
+    )
+    width = cross_cols.shape[1]
+    cross_two = jnp.concatenate(split_wide(cross_cols), axis=1)
+    both = contract_split(full_one, cross_two)
+    cov_cols = inv_one - (both[:, :width] + both[:, width:])
+    cov_two = jnp.concatenate(split_wide(cov_cols), axis=1)
+    both = contract_split(cov_two, full_parent) + contract_split(cross_two, full_root)
+    upper_rows = -(both[:width] + both[width:])
+    upper_cols = lax.all_to_all(
+        upper_rows.astype(bf16), "leaf", split_axis=1, concat_axis=0, tiled=True
+    )
+    child_cov = inv_two - (
+        contract_split(full_parent, upper_cols) + contract_split(full_root, lower_cols)
+    )
+    return (cross_rows, cov_cols, upper_rows, lower_rows, child_cov)
+
+
 def solution(mesh):
     placed = (
         P(("parts", "leaf"), None),
@@ -82,7 +371,7 @@
         P("parts", "leaf"),
     )
     return jax.shard_map(
-        per_device,
+        per_device_kernels if mesh.shape["leaf"] == GROUP else per_device,
         mesh=mesh,
         in_specs=placed,
         out_specs=(

time: 324 us -> 203 us (0.63)
  waiting for transfers between devices: 223 us -> 24.4 us
  Pallas kernels: 0 us -> 126 us
  matrix products: 58.7 us -> 17.7 us
  between operations: 14 us -> 0.85 us
    all_gather x3 -> x0, waiting for transfers between devices: 214 us -> none  [the longest x1 98.9 us: per_device(): lax.all_gather(masked_one, 'leaf', axis=0, tiled=True)]
    pallas_call x0 -> x1, Pallas kernels: none -> 126 us  [per_device_kernels(): pl.pallas_call(gather_kernel, out_shape=(jax.ShapeDtypeStruct((rows, pare...]
    dot_general x11 -> x5, matrix products: 58.7 us -> 17.7 us  [contract_split(): lax.dot_general(left, right, (((0,), (0,)), ((), ())), preferred_element_...]
    all_to_all x3, waiting for transfers between devices: 8.16 us -> 24.4 us  [the longest x1 16.1 us: per_device_kernels(): lax.all_to_all((cross_rows * CROSS_SCALE).astype(jnp.float16), 'leaf', sp...]
    unnamed x14 -> x18, local copies, waits for them, and re-layouts: 1.18 us -> 8.21 us
    select_n x6 -> x0, other arithmetic: 4.88 us -> none  [the longest x1 2.22 us: per_device(): masked_one = jnp.where(keep_one, panel_one, jnp.zeros_like(panel_one))]
  transfers between devices with their start and end apart: 6 -> 3, of which waited for: 4 -> 3; matrix products, arithmetic and copies ran while one was open for 18% -> 8% of each run, Pallas kernels for 0% -> 0%
where the time goes in v1:
time: 203 us; the launch traced here: 202 us
  Pallas kernels  126 us (62%)
  waiting for transfers between devices  24.4 us (12%)
  matrix products  17.7 us (9%)
  starting transfers between devices  16.2 us (8%)
  local copies, waits for them, and re-layouts  11.2 us (6%)
  other arithmetic  5.54 us (3%)
    pallas_call x1, Pallas kernels, per_device_kernels(): pl.pallas_call(gather_kernel, out_shape=(jax.ShapeDtypeStruct((rows, pare...  126 us
    dot_general x5, matrix products, contract_split(): lax.dot_general(left, right, (((0,), (0,)), ((), ())), preferred_element_...  17.7 us
    all_to_all x1, waiting for transfers between devices, per_device_kernels(): lax.all_to_all((cross_rows * CROSS_SCALE).astype(jnp.float16), 'leaf', sp...  16.1 us
    unnamed x18, local copies, waits for them, and re-layouts  8.21 us
    all_to_all x1, waiting for transfers between devices, per_device_kernels(): lax.all_to_all(upper_rows.astype(bf16), 'leaf', split_axis=1, concat_axis...  7.94 us
    all_to_all x1, starting transfers between devices, per_device_kernels(): lax.all_to_all(upper_rows.astype(bf16), 'leaf', split_axis=1, concat_axis...  5.73 us
    all_to_all x1, starting transfers between devices, per_device_kernels(): lax.all_to_all(lower_rows.astype(bf16), 'leaf', split_axis=1, concat_axis...  5.48 us
    all_to_all x1, starting transfers between devices, per_device_kernels(): lax.all_to_all((cross_rows * CROSS_SCALE).astype(jnp.float16), 'leaf', sp...  5.01 us
  transfers between devices with their start and end apart: 3, of which 3 were waited for; matrix products, arithmetic and copies ran while one was open for 8% of the time, Pallas kernels for 0%

profile of v1, /device:TPU:0, one launch (start us, length us, event | category | flops | bytes accessed | tf_op | source)
XLA Modules:
  0.0 202.1 jit_solution(968776066579449506)
XLA Ops:
  0.6 0.7 convert_element_type.32
  1.3 0.1 copy.17
  1.4 0.1 broadcast_in_dim.6
  1.5 0.7 copy.37
  2.3 0.7 convert_element_type.33
  3.0 0.1 copy.18
  3.0 0.1 broadcast_in_dim.7
  3.1 0.7 copy.38
  3.8 126.2 %gather_panels.1 = (f32[192,2048]{1,0:T(8,128)}, f32[192,1024]{1,0:T(8,128)}, bf16[3072,2048]{1,0:T(8,128)(2,1)}, bf16[3072,1024]{1,0:T(8,128)(2,1)}, bf16[2048,1024]{1,0:T(8,128)(2,1)}) custom-call(f32[192,3072]{1,0:T(8,128)} %root.1, bf16[192,2048]{1,0:T(8,128)(2,1)} %one_shard.1, bf16[192,1024]{1,0:T(8,128)(2,1)} %root_shard.1, ...), custom_call_target="tpu_custom_call" | custom-call | flops 7247757312 | bytes 300000000 | tf_op jit(solution)/shard_map/gather_panels/pallas_call | solution.py:317
  130.1 2.5 %copy_bitcast_fusion = f16[192,16,128]{2,0,1:T(8,128)(2,1)} fusion(f32[192,2048]{1,0:T(8,128)} %get-tuple-element.36), kind=kLoop, calls=%fused_computation.20 | loop fusion | flops 786432 | bytes 2359296 | tf_op jit(solution)/shard_map/all_to_all | solution.py:340
  132.6 0.0 copy-start.2
  132.6 5.0 %all-to-all-start = ((f16[192,16,128]{2,0,1:T(8,128)(2,1)}), f16[192,16,128]{2,0,1:T(8,128)(2,1)S(1)}, u32[]{:S(2)}, u32[]{:S(2)}) async-start(f16[192,16,128]{2,0,1:T(8,128)(2,1)} %copy_bitcast_fusion), calls=%async_computation | async-start | bytes 1572864 | tf_op jit(solution)/shard_map/all_to_all | solution.py:340
  137.6 1.6 copy.20
  139.2 0.0 copy-done.2
  139.2 0.1 convert_element_type.41
  139.2 1.0 copy.23
  140.2 16.1 %all-to-all-done = f16[192,16,128]{2,0,1:T(8,128)(2,1)S(1)} async-done(((f16[192,16,128]{2,0,1:T(8,128)(2,1)}), f16[192,16,128]{2,0,1:T(8,128)(2,1)S(1)}, u32[]{:S(2)}, u32[]{:S(2)}) %all-to-all-start) | async-done | bytes 786464 | tf_op jit(solution)/shard_map/all_to_all | solution.py:340
  156.3 5.5 %all-to-all-start.2 = ((bf16[192,16,64]{0,2,1:T(8,128)(2,1)}), bf16[192,16,64]{0,2,1:T(8,128)(2,1)S(1)}, u32[]{:S(2)}, u32[]{:S(2)}) async-start(bf16[192,16,64]{0,2,1:T(8,128)(2,1)} %bitcast.5), calls=%async_computation.2 | async-start | bytes 1048576 | tf_op jit(solution)/shard_map/all_to_all | solution.py:343
  161.8 0.2 convert_multiply_fusion
  162.0 0.0 slice-start
  162.0 0.2 reduce-precision_convert_fusion
  162.2 0.0 slice-start.1
  162.2 6.7 %fusion.8 = f32[2048,256]{0,1:T(8,128)S(1)} fusion(bf16[3072,2048]{1,0:T(8,128)(2,1)} %get-tuple-element.11, bf16[3072,128]{1,0:T(8,128)(2,1)S(1)} %get-tuple-element.30, bf16[3072,128]{1,0:T(8,128)(2,1)S(1)} %get-tuple-element.29), kind=kOutput, calls=%fused_computation.18 | convolution fusion | flops 3224371200 | bytes 16252928 | tf_op jit(solution)/shard_map/dot_general | solution.py:303
  168.9 0.0 copy-start.1
  168.9 0.2 reduce-precision_convert_fusion.1
  169.1 0.1 fusion.2
  169.2 1.8 copy-done.1
  171.1 1.3 fusion.4
  172.4 0.0 slice-done
  172.4 0.0 slice-done.1
  172.4 1.8 convolution_add_fusion
  174.2 0.9 fusion.17
  175.1 0.8 copy.21
  175.9 0.3 all-to-all-done.2
  176.3 5.7 %all-to-all-start.1 = ((bf16[128,16,64]{0,2,1:T(8,128)(2,1)}), bf16[128,16,64]{0,2,1:T(8,128)(2,1)}, u32[]{:S(2)}, u32[]{:S(2)}) async-start(bf16[128,16,64]{0,2,1:T(8,128)(2,1)} %bitcast.3), calls=%async_computation.1 | async-start | bytes 524288 | tf_op jit(solution)/shard_map/all_to_all | solution.py:353
  182.0 0.3 copy.24
  182.3 0.5 all_to_all.47
  182.9 1.3 copy.25
  184.2 0.0 copy-start.3
  184.2 7.9 %all-to-all-done.1 = bf16[128,16,64]{0,2,1:T(8,128)(2,1)} async-done(((bf16[128,16,64]{0,2,1:T(8,128)(2,1)}), bf16[128,16,64]{0,2,1:T(8,128)(2,1)}, u32[]{:S(2)}, u32[]{:S(2)}) %all-to-all-start.1) | async-done | bytes 262176 | tf_op jit(solution)/shard_map/all_to_all | solution.py:353
  192.1 3.1 %fusion.11 = f32[1024,64]{0,1:T(8,128)S(1)} fusion(bf16[2048,1024]{1,0:T(8,128)(2,1)} %get-tuple-element.12, bf16[128,16,64]{0,2,1:T(8,128)(2,1)} %all-to-all-done.1), kind=kOutput, calls=%fused_computation.23 | convolution fusion | flops 268435456 | bytes 4718592 | tf_op jit(solution)/shard_map/dot_general | solution.py:303
  195.2 0.0 copy-done.3
  195.2 0.0 copy-start
  195.2 4.8 %fusion.1 = f32[1024,64]{0,1:T(8,128)} fusion(f32[1024,64]{0,1:T(8,128)S(1)} %copy-done.3, f32[1024,64]{0,1:T(8,128)S(1)} %fusion.11, bf16[3072,64]{0,1:T(8,128)(2,1)S(1)} %all_to_all.47, bf16[3072,1024]{1,0:T(8,128)(2,1)} %get-tuple-element.13), kind=kOutput, calls=%fused_computation.10 | convolution fusion | flops 402784256 | bytes 7471104 | tf_op jit(solution)/shard_map/dot_general | solution.py:303
  200.1 0.0 copy-done
  200.1 1.1 copy.41
  201.2 0.9 copy.42
  (1 shorter events, 0.0 us)
Async XLA Ops:
  132.6 6.6 %copy-start.2 = (f32[192,1024]{1,0:T(8,128)S(1)}, f32[192,1024]{1,0:T(8,128)}, u32[]{:S(2)}) copy-start(f32[192,1024]{1,0:T(8,128)} %get-tuple-element.39) | copy-start | bytes 2359300
  132.6 23.7 %all-to-all-start = ((f16[192,16,128]{2,0,1:T(8,128)(2,1)}), f16[192,16,128]{2,0,1:T(8,128)(2,1)S(1)}, u32[]{:S(2)}, u32[]{:S(2)}) async-start(f16[192,16,128]{2,0,1:T(8,128)(2,1)} %copy_bitcast_fusion), calls=%async_computation | async-start | bytes 1572864 | tf_op jit(solution)/shard_map/all_to_all | solution.py:340
  156.3 20.0 %all-to-all-start.2 = ((bf16[192,16,64]{0,2,1:T(8,128)(2,1)}), bf16[192,16,64]{0,2,1:T(8,128)(2,1)S(1)}, u32[]{:S(2)}, u32[]{:S(2)}) async-start(bf16[192,16,64]{0,2,1:T(8,128)(2,1)} %bitcast.5), calls=%async_computation.2 | async-start | bytes 1048576 | tf_op jit(solution)/shard_map/all_to_all | solution.py:343
  162.0 10.4 %slice-start = ((s8[6291456]{0:T(1024)(128)(4,1)}), s8[4194304]{0:T(1024)(128)(4,1)S(1)}, s32[]{:S(2)}) async-start(s8[6291456]{0:T(1024)(128)(4,1)} %bitcast.37), calls=%async_computation.3 | async-start | bytes 8388608
  162.2 10.1 %slice-start.1 = ((s8[6291456]{0:T(1024)(128)(4,1)}), s8[2097152]{0:T(1024)(128)(4,1)S(1)}, s32[]{:S(2)}) async-start(s8[6291456]{0:T(1024)(128)(4,1)} %bitcast.37), calls=%async_computation.4 | async-start | bytes 4194304
  168.9 2.2 %copy-start.1 = (bf16[2048,1024]{1,0:T(8,128)(2,1)S(1)}, bf16[2048,1024]{1,0:T(8,128)(2,1)}, u32[]{:S(2)}) copy-start(bf16[2048,1024]{1,0:T(8,128)(2,1)} %get-tuple-element.12) | copy-start | bytes 12582916
  176.3 15.8 %all-to-all-start.1 = ((bf16[128,16,64]{0,2,1:T(8,128)(2,1)}), bf16[128,16,64]{0,2,1:T(8,128)(2,1)}, u32[]{:S(2)}, u32[]{:S(2)}) async-start(bf16[128,16,64]{0,2,1:T(8,128)(2,1)} %bitcast.3), calls=%async_computation.1 | async-start | bytes 524288 | tf_op jit(solution)/shard_map/all_to_all | solution.py:353
  184.2 11.1 %copy-start.3 = (f32[1024,64]{0,1:T(8,128)S(1)}, f32[1024,64]{0,1:T(8,128)}, u32[]{:S(2)}) copy-start(f32[1024,64]{0,1:T(8,128)} %param.15) | copy-start | bytes 786436
  195.2 4.8 %copy-start = (f32[192,2048]{1,0:T(8,128)S(1)}, f32[192,2048]{1,0:T(8,128)}, u32[]{:S(2)}) copy-start(f32[192,2048]{1,0:T(8,128)} %get-tuple-element.36) | copy-start | bytes 4718596
